TPU v7x, 32 devices: a whole 2x2x4 slice. The times are simulated.
32 devices in a mesh: depth: 8 (over z, y), lat: 4 (over x, core).
Axes of the slice: x: 2, y: 2, z: 4, core: 2. Of those that a mesh axis runs over, the one named last changes fastest.
Arguments:
- object_slices: float32 [8, 2, 512, 2048], P('depth', None, 'lat'), as said below
- probe: float32 [2, 2, 256, 256], replicated, may hold values from -2.7 to 2.7
- positions: int32 [16, 2], P('lat'), may hold values from 0 to 1792, as said below
- measured: float32 [16, 256, 256], P('lat'), may hold values from 0 to 0.8
Outputs:
- object_grad: float32 [8, 2, 512, 2048], P('depth', None, 'lat')
Inputs may be any that keep to these rules, and one draw needn't show every extreme that they name: Rows 4 l ... 4 l + 3 are the positions of lat index l: their row offset lies in [l * 128, (l + 1) * 128) and their column offset in [0, 1792]. `object_slices`: each cell's magnitude, sqrt(real part squared plus imaginary part squared), lies between 0.9 and 1.
All inputs are finite; a program needn't handle non-finite values.
Results may differ from a plain program's by a relative error of at most 0.039.
Values may be sent and summed in bfloat16 or wider, within the bound.
A program may use at most 64 MiB of HBM per device.

v0:
```python
import functools
import math

import jax
import jax.numpy as jnp
import ml_dtypes
import numpy as np
from jax import lax
from jax.experimental import pallas as pl
from jax.experimental.pallas import tpu as pltpu
from jax.sharding import PartitionSpec as P

fresnel = 0.5
MESH = pl.DeviceIdType.MESH
TILES = 3
SENT = 2
LANES = 128
VMEM_BYTES = 48 * 1024 * 1024


def shifted(block, axis, distance):
    devices = range(lax.axis_size(axis))
    route = [((i - distance) % len(devices), i) for i in devices]
    return lax.ppermute(block, axis, route)


def host_tables(pixels):
    idx = np.arange(pixels)
    angle = 2.0 * np.pi * (np.outer(idx, idx) % pixels) / pixels
    far = np.exp(-1j * angle) / math.sqrt(pixels)
    freq = np.where(idx < pixels // 2, idx, idx - pixels).astype(np.float64)
    prop = (np.conj(far) * np.exp(-1j * np.pi * fresnel * freq * freq / pixels)[None, :]) @ far

    def block(table):
        return np.block([[table.real, -table.imag], [table.imag, table.real]])

    prop_block, far_block = block(prop), block(far)
    tables = np.stack([prop_block, prop_block.T, far_block, far_block.T])
    high = tables.astype(ml_dtypes.bfloat16)
    rest = (tables - high.astype(np.float64)).astype(ml_dtypes.bfloat16)
    return jnp.asarray(np.stack([high, rest], axis=1))


def window_place(positions_ref, k, tile_rows, col_tiles):
    row = lax.rem(positions_ref[k, 0], tile_rows)
    col = positions_ref[k, 1]
    first = jnp.minimum(col // LANES, col_tiles - 3)
    return row, first, col - first * LANES


def upper_rows(shape, keep):
    return lax.broadcasted_iota(jnp.int32, shape, 0) < keep


def extract_kernel(near0_ref, near1_ref, near2_ref, tile_ref, blocks_ref):
    near = (near0_ref, near1_ref, near2_ref)
    _, _, tile_rows, cols = tile_ref.shape
    _, count, _, _, pixels = blocks_ref.shape
    wide = pixels + LANES

    for j in range(TILES):

        @pl.loop(0, count)
        def _(k):
            row, first, shift = window_place(near[j], k, tile_rows, cols // LANES)
            start = pl.multiple_of(first * LANES, LANES)
            for part in range(2):
                piece = tile_ref[0, part, :, pl.ds(start, wide)]
                piece = pltpu.roll(piece, lax.rem(wide - shift, wide), 1)[:, :pixels]
                piece = pltpu.roll(piece, lax.rem(tile_rows - row, tile_rows), 0)
                blocks_ref[j, k, part] = piece.astype(blocks_ref.dtype)


def gather_kernel(near0_ref, near1_ref, near2_ref, terms_ref, grad_ref):
    near = (near0_ref, near1_ref, near2_ref)
    _, _, tile_rows, cols = grad_ref.shape
    _, count, _, _, pixels = terms_ref.shape
    wide = pixels + LANES
    grad_ref[...] = jnp.zeros_like(grad_ref)

    for j in range(TILES):

        @pl.loop(0, count)
        def _(k):
            row, first, shift = window_place(near[j], k, tile_rows, cols // LANES)
            start = pl.multiple_of(first * LANES, LANES)
            for part in range(2):
                piece = terms_ref[j, k, part].astype(jnp.float32)
                if j != 1:
                    upper = upper_rows(piece.shape, tile_rows - row)
                    kept = upper if j == 0 else jnp.logical_not(upper)
                    piece = jnp.where(kept, piece, 0.0)
                piece = pltpu.roll(piece, row, 0)
                piece = jnp.concatenate(
                    [piece, jnp.zeros((tile_rows, LANES), jnp.float32)], axis=1
                )
                piece = pltpu.roll(piece, shift, 1)
                grad_ref[0, part, :, pl.ds(start, wide)] += piece


def spread(count, sections, lats):
    stride = sections // count
    me = lax.axis_index("depth")
    lat = lax.axis_index("lat")
    works = (lax.rem(me, stride) == lax.rem(lat, stride)) & (me // stride < count)
    return stride, me, lat, works


def worker_of(j, k, lat, lats, stride):
    owner = lax.rem(lat - j + lats, lats)
    return {"depth": k * stride + lax.rem(owner, stride), "lat": owner}


def transform(left, right, parts, pixels):
    low = jnp.bfloat16
    stacked = jnp.concatenate(
        [jnp.concatenate([p.astype(low) for p in pair], axis=0) for pair in parts], axis=1
    )
    dot = functools.partial(jnp.dot, preferred_element_type=jnp.float32)
    middle = (dot(left[0], stacked) + dot(left[1], stacked)).astype(low)
    rows = [
        jnp.concatenate(
            [
                middle[:pixels, m * pixels : (m + 1) * pixels],
                middle[pixels:, m * pixels : (m + 1) * pixels],
            ],
            axis=1,
        )
        for m in range(len(parts))
    ]
    joined = jnp.concatenate(rows, axis=0)
    ended = dot(joined, right[0]) + dot(joined, right[1])
    return [
        (
            ended[m * pixels : (m + 1) * pixels, :pixels],
            ended[m * pixels : (m + 1) * pixels, pixels:],
        )
        for m in range(len(parts))
    ]


def main_kernel(
    count,
    sections,
    lats,
    near0_ref,
    blocks,
    probe_ref,
    measured_ref,
    tables_ref,
    terms_ref,
    merged,
    halo,
    held,
    made,
    saved,
    back,
    tables,
    start_wave,
    target,
    load_sem,
    out_sem,
    in_sem,
    own_sem,
    made_sem,
    terms_sem,
    halo_out_sem,
    halo_in_sem,
    pass_sem,
):
    tile_rows, pixels = held.shape[3:]
    modes = probe_ref.shape[0]
    stride, me, lat, works = spread(count, sections, lats)
    window = lax.rem(me // stride, count)

    def source(s, j):
        return {"depth": s, "lat": lax.rem(lat + j, lats)}

    def mine(j, k):
        return works & (window == k) if j == 0 else False

    barrier = pltpu.get_barrier_semaphore()
    for j in range(SENT):

        @pl.loop(0, count)
        def _(k):
            @pl.when(jnp.logical_not(mine(j, k)))
            def _():
                pl.semaphore_signal(
                    barrier,
                    inc=1,
                    device_id=worker_of(j, k, lat, lats, stride),
                    device_id_type=MESH,
                )

    ahead = {"depth": me, "lat": lax.rem(lat + 2, lats)}
    behind = {"depth": me, "lat": lax.rem(lat - 2 + lats, lats)}
    for peer in (ahead, behind):
        pl.semaphore_signal(barrier, inc=1, device_id=peer, device_id_type=MESH)

    loads = (
        pltpu.make_async_copy(tables_ref, tables, load_sem.at[0]),
        pltpu.make_async_copy(probe_ref, start_wave, load_sem.at[1]),
        pltpu.make_async_copy(measured_ref.at[window], target, load_sem.at[2]),
    )

    @pl.when(works)
    def _():
        for j in range(SENT):

            @pl.loop(0, sections)
            def _(s):
                @pl.when((s != me) if j == 0 else True)
                def _():
                    pl.semaphore_signal(
                        barrier, inc=1, device_id=source(s, j), device_id_type=MESH
                    )

        for load in loads:
            load.start()

    busy = works.astype(jnp.int32)
    pl.semaphore_wait(barrier, SENT * count + 2 - busy + busy * (SENT * sections - 1))

    def block_out(j, k):
        return pltpu.make_async_remote_copy(
            src_ref=merged.at[k] if j == 0 else blocks.at[j, k],
            dst_ref=held.at[me, j],
            send_sem=out_sem.at[j, k],
            recv_sem=in_sem.at[me, j],
            device_id=worker_of(j, k, lat, lats, stride),
            device_id_type=MESH,
        )

    def block_own(k):
        return pltpu.make_async_copy(merged.at[k], held.at[me, 0], own_sem.at[0])

    far_first = 1 - jnp.minimum((4 * me) // sections, 1)

    def order(turn):
        return far_first * (count - 1 - turn) + (1 - far_first) * turn

    def rows_out(k):
        return pltpu.make_async_remote_copy(
            src_ref=blocks.at[2, k],
            dst_ref=halo.at[k],
            send_sem=halo_out_sem.at[k],
            recv_sem=halo_in_sem.at[k],
            device_id=behind,
            device_id_type=MESH,
        )

    @pl.loop(0, count)
    def _(turn):
        rows_out(order(turn)).start()

    @pl.loop(0, count)
    def _(turn):
        block_out(1, order(turn)).start()

    def upper(k):
        keep = tile_rows - lax.rem(near0_ref[k, 0], tile_rows)
        return upper_rows((tile_rows, pixels), keep)

    @pl.loop(0, count)
    def _(turn):
        k = order(turn)
        rows_out(k).wait_recv()
        for part in range(2):
            merged[k, part] = jnp.where(
                upper(k),
                blocks[0, k, part].astype(jnp.float32),
                halo[k, part].astype(jnp.float32),
            ).astype(merged.dtype)
        own = mine(0, k)

        @pl.when(own)
        def _():
            block_own(k).start()

        @pl.when(jnp.logical_not(own))
        def _():
            block_out(0, k).start()

    def term_out(s, j):
        return pltpu.make_async_remote_copy(
            src_ref=made.at[s, j],
            dst_ref=terms_ref.at[j, window],
            send_sem=made_sem.at[s, j],
            recv_sem=terms_sem.at[j, window],
            device_id=source(s, j),
            device_id_type=MESH,
        )

    def term_own():
        return pltpu.make_async_copy(
            made.at[me, 0], terms_ref.at[0, window], own_sem.at[1]
        )

    def patch(s):
        mask = upper(window)
        out = []
        for part in range(2):
            a, b = (held[s, j, part].astype(jnp.float32) for j in range(SENT))
            out.append(
                jnp.concatenate([jnp.where(mask, a, b), jnp.where(mask, b, a)], axis=0)
            )
        return out

    @pl.when(works)
    def _():
        for load in loads:
            load.wait()
        saved[0] = start_wave[...].astype(jnp.bfloat16)
        block_own(window).wait()

        @pl.loop(0, sections)
        def _(s):
            for j in range(SENT):

                @pl.when((s != me) if j == 0 else True)
                def _():
                    pltpu.make_async_remote_copy(
                        src_ref=blocks.at[0, 0],
                        dst_ref=held.at[s, j],
                        send_sem=out_sem.at[0, 0],
                        recv_sem=in_sem.at[s, j],
                        device_id=source(s, j),
                        device_id_type=MESH,
                    ).wait_recv()

            p_real, p_imag = patch(s)
            lit = []
            for m in range(modes):
                w_real = saved[s, m, 0].astype(jnp.float32)
                w_imag = saved[s, m, 1].astype(jnp.float32)
                lit.append(
                    (p_real * w_real - p_imag * w_imag, p_real * w_imag + p_imag * w_real)
                )
            moved = transform(tables.at[0], tables.at[1], lit, pixels)
            for m in range(modes):
                for part in range(2):
                    saved[s + 1, m, part] = moved[m][part].astype(jnp.bfloat16)

        last = [(saved[sections, m, 0], saved[sections, m, 1]) for m in range(modes)]
        far = transform(tables.at[2], tables.at[3], last, pixels)
        resid = -target[...]
        for real, imag in far:
            resid = resid + (real * real + imag * imag)
        seed = [(resid * real, resid * imag) for real, imag in far]
        seed = transform(tables.at[3], tables.at[2], seed, pixels)
        for m in range(modes):
            for part in range(2):
                back[m, part] = seed[m][part].astype(jnp.bfloat16)

        @pl.loop(0, sections)
        def _(step):
            s = sections - 1 - step
            p_real, p_imag = patch(s)
            waves = [(back[m, 0], back[m, 1]) for m in range(modes)]
            lit = transform(tables.at[1], tables.at[0], waves, pixels)
            g_real = jnp.zeros((pixels, pixels), jnp.float32)
            g_imag = jnp.zeros((pixels, pixels), jnp.float32)
            for m in range(modes):
                l_real, l_imag = lit[m]
                w_real = saved[s, m, 0].astype(jnp.float32)
                w_imag = saved[s, m, 1].astype(jnp.float32)
                g_real = g_real + (w_real * l_real + w_imag * l_imag)
                g_imag = g_imag + (w_real * l_imag - w_imag * l_real)
                back[m, 0] = (p_real * l_real + p_imag * l_imag).astype(jnp.bfloat16)
                back[m, 1] = (p_real * l_imag - p_imag * l_real).astype(jnp.bfloat16)
            mask = upper(window)
            for part, term in enumerate((g_real, g_imag)):
                top, bottom = term[:tile_rows], term[tile_rows:]
                made[s, 0, part] = jnp.where(mask, top, bottom).astype(made.dtype)
                made[s, 1, part] = jnp.where(mask, bottom, top).astype(made.dtype)
            for j in range(SENT):

                @pl.when((s != me) if j == 0 else True)
                def _():
                    term_out(s, j).start()

            @pl.when(s == me)
            def _():
                term_own().start()

        term_own().wait()

    def arrived(j, k):
        return pltpu.make_async_remote_copy(
            src_ref=made.at[0, 0],
            dst_ref=terms_ref.at[j, k],
            send_sem=made_sem.at[0, 0],
            recv_sem=terms_sem.at[j, k],
            device_id=worker_of(j, k, lat, lats, stride),
            device_id_type=MESH,
        )

    def pass_on(k):
        return pltpu.make_async_remote_copy(
            src_ref=terms_ref.at[0, k],
            dst_ref=terms_ref.at[2, k],
            send_sem=pass_sem.at[k],
            recv_sem=terms_sem.at[2, k],
            device_id=ahead,
            device_id_type=MESH,
        )

    upper_half = (2 * me) // sections

    def back_order(turn):
        return upper_half * (count - 1 - turn) + (1 - upper_half) * turn

    @pl.loop(0, count)
    def _(turn):
        k = back_order(turn)

        @pl.when(jnp.logical_not(mine(0, k)))
        def _():
            arrived(0, k).wait_recv()

        pass_on(k).start()

    @pl.when(works)
    def _():
        @pl.loop(0, sections)
        def _(s):
            for j in range(SENT):

                @pl.when((s != me) if j == 0 else True)
                def _():
                    term_out(s, j).wait_send()

    @pl.loop(0, count)
    def _(k):
        rows_out(k).wait_send()
        block_out(1, k).wait_send()
        arrived(1, k).wait_recv()
        pass_on(k).wait()

        @pl.when(jnp.logical_not(mine(0, k)))
        def _():
            block_out(0, k).wait_send()


def on_device(object_slices, probe, positions, measured):
    pixels = probe.shape[-1]
    tile_rows, cols = object_slices.shape[2:]
    count = positions.shape[0]
    sections = lax.axis_size("depth")
    lats = lax.axis_size("lat")
    low = jnp.bfloat16
    vmem = pl.BlockSpec(memory_space=pltpu.VMEM)
    smem = pl.BlockSpec(memory_space=pltpu.SMEM)
    anywhere = pl.BlockSpec(memory_space=pl.ANY)
    block = (2, tile_rows, pixels)
    tables = host_tables(pixels)
    near = [positions] + [shifted(positions, "lat", j) for j in range(1, TILES)]

    blocks = pl.pallas_call(
        extract_kernel,
        out_shape=jax.ShapeDtypeStruct((TILES, count) + block, low),
        in_specs=[smem] * TILES + [vmem],
        out_specs=vmem,
        compiler_params=pltpu.CompilerParams(vmem_limit_bytes=VMEM_BYTES),
        name="extract",
    )(*near, object_slices)

    terms = pl.pallas_call(
        functools.partial(main_kernel, count, sections, lats),
        out_shape=jax.ShapeDtypeStruct((TILES, count) + block, low),
        in_specs=[smem, vmem] + [anywhere] * 3,
        out_specs=anywhere,
        scratch_shapes=[
            pltpu.VMEM((count,) + block, low),
            pltpu.VMEM((count,) + block, low),
            pltpu.VMEM((sections, SENT) + block, low),
            pltpu.VMEM((sections, SENT) + block, low),
            pltpu.VMEM((sections + 1,) + probe.shape, low),
            pltpu.VMEM(probe.shape, low),
            pltpu.VMEM(tables.shape, low),
            pltpu.VMEM(probe.shape, jnp.float32),
            pltpu.VMEM(measured.shape[1:], jnp.float32),
            pltpu.SemaphoreType.DMA((3,)),
            pltpu.SemaphoreType.DMA((SENT, count)),
            pltpu.SemaphoreType.DMA((sections, SENT)),
            pltpu.SemaphoreType.DMA((2,)),
            pltpu.SemaphoreType.DMA((sections, SENT)),
            pltpu.SemaphoreType.DMA((TILES, count)),
            pltpu.SemaphoreType.DMA((count,)),
            pltpu.SemaphoreType.DMA((count,)),
            pltpu.SemaphoreType.DMA((count,)),
        ],
        compiler_params=pltpu.CompilerParams(
            collective_id=0, has_side_effects=True, vmem_limit_bytes=VMEM_BYTES
        ),
        name="windows",
    )(positions, blocks, probe, measured, tables)

    return pl.pallas_call(
        gather_kernel,
        out_shape=jax.ShapeDtypeStruct(object_slices.shape, jnp.float32),
        in_specs=[smem] * TILES + [vmem],
        out_specs=vmem,
        compiler_params=pltpu.CompilerParams(vmem_limit_bytes=VMEM_BYTES),
        name="gather",
    )(*near, terms)


def solution(mesh):
    return jax.shard_map(
        on_device,
        mesh=mesh,
        in_specs=(P("depth", None, "lat", None), P(), P("lat", None), P("lat", None, None)),
        out_specs=P("depth", None, "lat", None),
        check_vma=False,
    )
```

profile of v0, /device:TPU:0, one launch (start us, length us, event | category | flops | bytes accessed | tf_op | source)
XLA Modules:
  0.0 91.7 jit_solution(10955907448329034524)
XLA Ops:
  0.0 0.8 copy.10.near0_ref
  0.8 2.9 %collective-permute-start.1 = (s32[4,2]{1,0:T(4,128)S(1)}, s32[4,2]{1,0:T(4,128)S(1)}, u32[]{:S(2)}, u32[]{:S(2)}) collective-permute-start(s32[4,2]{1,0:T(4,128)S(1)} %copy.10.near0_ref), channel_id=1, source_target_pairs={{2,0},{3,1},{0,2},{1,3},{6,4},{7,5},{4,6},{5,7},{10,8},{11,9},{8,1... | collective-permute-start | bytes 104 | tf_op jit(solution)/shard_map/ppermute | solution.py:24
  3.7 0.0 collective-permute-start
  3.7 1.6 %collective-permute-done.1.near2_ref = s32[4,2]{1,0:T(4,128)S(1)} collective-permute-done((s32[4,2]{1,0:T(4,128)S(1)}, s32[4,2]{1,0:T(4,128)S(1)}, u32[]{:S(2)}, u32[]{:S(2)}) %collective-permute-start.1) | collective-permute-done | bytes 64 | tf_op jit(solution)/shard_map/ppermute | solution.py:24
  5.3 1.4 %collective-permute-done.near1_ref = s32[4,2]{1,0:T(4,128)S(1)} collective-permute-done((s32[4,2]{1,0:T(4,128)S(1)}, s32[4,2]{1,0:T(4,128)S(1)}, u32[]{:S(2)}, u32[]{:S(2)}) %collective-permute-start) | collective-permute-done | bytes 64 | tf_op jit(solution)/shard_map/ppermute | solution.py:24
  6.7 0.0 copy-start
  6.7 1.6 %copy-done = f32[1,2,128,2048]{3,2,1,0:T(8,128)S(1)} copy-done((f32[1,2,128,2048]{3,2,1,0:T(8,128)S(1)}, f32[1,2,128,2048]{3,2,1,0:T(8,128)}, u32[]{:S(2)}) %copy-start) | copy-done | bytes 2097176
  8.3 0.0 copy-start.1
  8.3 0.0 copy-start.2
  8.3 3.2 %extract.1.blocks = bf16[3,4,2,128,256]{4,3,2,1,0:T(8,128)(2,1)S(1)} custom-call(s32[4,2]{1,0:T(4,128)S(1)} %copy.10.near0_ref, s32[4,2]{1,0:T(4,128)S(1)} %collective-permute-done.near1_ref, s32[4,2]{1,0:T(4,128)S(1)} %collective-permute-done.1.near2_ref, f32[1,2,128,2048]{3,2,1,0:T(8,128)S(1)} %copy-done), custom_call_target="tpu_custom_call" | custom-call | tf_op jit(solution)/shard_map/extract/pallas_call | solution.py:460
  11.5 0.0 copy-done.1
  11.5 0.0 copy-done.2
  11.5 75.5 %windows.1.terms_ref = bf16[3,4,2,128,256]{4,3,2,1,0:T(8,128)(2,1)S(1)} custom-call(s32[4,2]{1,0:T(4,128)S(1)} %copy.10.near0_ref, bf16[3,4,2,128,256]{4,3,2,1,0:T(8,128)(2,1)S(1)} %extract.1.blocks, f32[2,2,256,256]{3,2,1,0:T(8,128)S(1)} %copy-done.1, f32[4,256,256]{2,1,0:T(8,128)S(1)} %copy-done.2, bf16[4,2,512,512]{3,2,1,0:T(8,128)(2,1)} %constant.2.clone.tables_ref), custom_call_target="tpu_custom_call" | custom-call | tf_op jit(solution)/shard_map/windows/pallas_call | solution.py:469
  87.0 4.6 %gather.1 = f32[1,2,128,2048]{3,2,1,0:T(8,128)} custom-call(s32[4,2]{1,0:T(4,128)S(1)} %copy.10.near0_ref, s32[4,2]{1,0:T(4,128)S(1)} %collective-permute-done.near1_ref, s32[4,2]{1,0:T(4,128)S(1)} %collective-permute-done.1.near2_ref, bf16[3,4,2,128,256]{4,3,2,1,0:T(8,128)(2,1)S(1)} %windows.1.terms_ref), custom_call_target="tpu_custom_call" | custom-call | tf_op jit(solution)/shard_map/gather/pallas_call | solution.py:500
Async XLA Ops:
  0.8 4.5 %collective-permute-start.1 = (s32[4,2]{1,0:T(4,128)S(1)}, s32[4,2]{1,0:T(4,128)S(1)}, u32[]{:S(2)}, u32[]{:S(2)}) collective-permute-start(s32[4,2]{1,0:T(4,128)S(1)} %copy.10.near0_ref), channel_id=1, source_target_pairs={{2,0},{3,1},{0,2},{1,3},{6,4},{7,5},{4,6},{5,7},{10,8},{11,9},{8,1... | collective-permute-start | bytes 104 | tf_op jit(solution)/shard_map/ppermute | solution.py:24
  3.7 3.0 %collective-permute-start = (s32[4,2]{1,0:T(4,128)S(1)}, s32[4,2]{1,0:T(4,128)S(1)}, u32[]{:S(2)}, u32[]{:S(2)}) collective-permute-start(s32[4,2]{1,0:T(4,128)S(1)} %copy.10.near0_ref), channel_id=1, source_target_pairs={{3,0},{0,1},{1,2},{2,3},{7,4},{4,5},{5,6},{6,7},{11,8},{8,9},{9,10... | collective-permute-start | bytes 104 | tf_op jit(solution)/shard_map/ppermute | solution.py:24
  6.7 1.6 %copy-start = (f32[1,2,128,2048]{3,2,1,0:T(8,128)S(1)}, f32[1,2,128,2048]{3,2,1,0:T(8,128)}, u32[]{:S(2)}) copy-start(f32[1,2,128,2048]{3,2,1,0:T(8,128)} %tile_ref.1) | copy-start | bytes 6291460
  8.3 3.2 %copy-start.1 = (f32[2,2,256,256]{3,2,1,0:T(8,128)S(1)}, f32[2,2,256,256]{3,2,1,0:T(8,128)}, u32[]{:S(2)}) copy-start(f32[2,2,256,256]{3,2,1,0:T(8,128)} %probe_ref.1) | copy-start | bytes 3145732
  8.3 3.2 %copy-start.2 = (f32[4,256,256]{2,1,0:T(8,128)S(1)}, f32[4,256,256]{2,1,0:T(8,128)}, u32[]{:S(2)}) copy-start(f32[4,256,256]{2,1,0:T(8,128)} %measured_ref.1) | copy-start | bytes 3145732
where the time goes:
time: 91.8 us; the launch traced here: 91.7 us
  Pallas kernels  83.3 us (91%)
  waiting for transfers between devices  3.01 us (3%)
  starting transfers between devices  2.94 us (3%)
  local copies, waits for them, and re-layouts  2.36 us (3%)
    pallas_call x1, Pallas kernels, on_device(): pl.pallas_call(functools.partial(main_kernel, count, sections, lats), out...  75.5 us
    pallas_call x1, Pallas kernels, on_device(): pl.pallas_call(gather_kernel, out_shape=jax.ShapeDtypeStruct(object_slice...  4.63 us
    pallas_call x1, Pallas kernels, on_device(): pl.pallas_call(extract_kernel, out_shape=jax.ShapeDtypeStruct((TILES, cou...  3.19 us
    ppermute x2, waiting for transfers between devices, shifted(): return lax.ppermute(block, axis, route)  3.01 us
    ppermute x2, starting transfers between devices, shifted(): return lax.ppermute(block, axis, route)  2.94 us
    unnamed x7, local copies, waits for them, and re-layouts  2.36 us
  transfers between devices with their start and end apart: 2, of which 2 were waited for; matrix products, arithmetic and copies ran while one was open for 0% of the time, Pallas kernels for 0%

commit v1 on v0

--- a/solution.py
+++ b/solution.py
@@ -52,13 +52,13 @@
     return lax.broadcasted_iota(jnp.int32, shape, 0) < keep
 
 
-def extract_kernel(near0_ref, near1_ref, near2_ref, tile_ref, blocks_ref):
-    near = (near0_ref, near1_ref, near2_ref)
+def extract_kernel(*refs):
+    *near, tile_ref, blocks_ref = refs
     _, _, tile_rows, cols = tile_ref.shape
     _, count, _, _, pixels = blocks_ref.shape
     wide = pixels + LANES
 
-    for j in range(TILES):
+    for j in range(len(near)):
 
         @pl.loop(0, count)
         def _(k):
@@ -144,6 +144,7 @@
     sections,
     lats,
     near0_ref,
+    own_blocks,
     blocks,
     probe_ref,
     measured_ref,
@@ -224,7 +225,7 @@
 
     def block_out(j, k):
         return pltpu.make_async_remote_copy(
-            src_ref=merged.at[k] if j == 0 else blocks.at[j, k],
+            src_ref=merged.at[k] if j == 0 else blocks.at[j - 1, k],
             dst_ref=held.at[me, j],
             send_sem=out_sem.at[j, k],
             recv_sem=in_sem.at[me, j],
@@ -242,7 +243,7 @@
 
     def rows_out(k):
         return pltpu.make_async_remote_copy(
-            src_ref=blocks.at[2, k],
+            src_ref=blocks.at[1, k],
             dst_ref=halo.at[k],
             send_sem=halo_out_sem.at[k],
             recv_sem=halo_in_sem.at[k],
@@ -269,7 +270,7 @@
         for part in range(2):
             merged[k, part] = jnp.where(
                 upper(k),
-                blocks[0, k, part].astype(jnp.float32),
+                own_blocks[0, k, part].astype(jnp.float32),
                 halo[k, part].astype(jnp.float32),
             ).astype(merged.dtype)
         own = mine(0, k)
@@ -457,19 +458,26 @@
     tables = host_tables(pixels)
     near = [positions] + [shifted(positions, "lat", j) for j in range(1, TILES)]
 
-    blocks = pl.pallas_call(
-        extract_kernel,
-        out_shape=jax.ShapeDtypeStruct((TILES, count) + block, low),
-        in_specs=[smem] * TILES + [vmem],
-        out_specs=vmem,
-        compiler_params=pltpu.CompilerParams(vmem_limit_bytes=VMEM_BYTES),
-        name="extract",
-    )(*near, object_slices)
+    def extract(places):
+        return pl.pallas_call(
+            extract_kernel,
+            out_shape=jax.ShapeDtypeStruct((len(places), count) + block, low),
+            in_specs=[smem] * len(places) + [vmem],
+            out_specs=vmem,
+            compiler_params=pltpu.CompilerParams(vmem_limit_bytes=VMEM_BYTES),
+            cost_estimate=pl.CostEstimate(
+                flops=0, bytes_accessed=4 * object_slices[0].size, transcendentals=0
+            ),
+            name="extract",
+        )(*places, object_slices)
+
+    own_blocks = extract(near[:1])
+    blocks = extract(near[1:])
 
     terms = pl.pallas_call(
         functools.partial(main_kernel, count, sections, lats),
         out_shape=jax.ShapeDtypeStruct((TILES, count) + block, low),
-        in_specs=[smem, vmem] + [anywhere] * 3,
+        in_specs=[smem, vmem, vmem] + [anywhere] * 3,
         out_specs=anywhere,
         scratch_shapes=[
             pltpu.VMEM((count,) + block, low),
@@ -495,7 +503,7 @@
             collective_id=0, has_side_effects=True, vmem_limit_bytes=VMEM_BYTES
         ),
         name="windows",
-    )(positions, blocks, probe, measured, tables)
+    )(positions, own_blocks, blocks, probe, measured, tables)
 
     return pl.pallas_call(
         gather_kernel,

time: 91.8 us -> 91.5 us (level)
  waiting for transfers between devices: 3.01 us -> 0.01 us
  Pallas kernels: 83.3 us -> 85.8 us
    ppermute x2, waiting for transfers between devices: 3.01 us -> 0.01 us  [shifted(): return lax.ppermute(block, axis, route)]
    pallas_call x1, Pallas kernels: 75.5 us -> 77.5 us  [on_device(): pl.pallas_call(functools.partial(main_kernel, count, sections, lats), out...]
    pallas_call x1 -> x2, Pallas kernels: 3.19 us -> 3.72 us  [extract(): pl.pallas_call(extract_kernel, out_shape=jax.ShapeDtypeStruct((len(places...]
    unnamed x7 -> x9, local copies, waits for them, and re-layouts: 2.36 us -> 2.49 us
  transfers between devices with their start and end apart: 2 -> 2, of which waited for: 2 -> 0; matrix products, arithmetic and copies ran while one was open for 0% -> 0% of each run, Pallas kernels for 0% -> 2%
where the time goes in v1:
time: 91.5 us; the launch traced here: 91.3 us
  Pallas kernels  85.8 us (94%)
  starting transfers between devices  2.94 us (3%)
  local copies, waits for them, and re-layouts  2.49 us (3%)
    pallas_call x1, Pallas kernels, on_device(): pl.pallas_call(functools.partial(main_kernel, count, sections, lats), out...  77.5 us
    pallas_call x1, Pallas kernels, on_device(): pl.pallas_call(gather_kernel, out_shape=jax.ShapeDtypeStruct(object_slice...  4.63 us
    pallas_call x2, Pallas kernels, extract(): pl.pallas_call(extract_kernel, out_shape=jax.ShapeDtypeStruct((len(places...  3.72 us
    ppermute x2, starting transfers between devices, shifted(): return lax.ppermute(block, axis, route)  2.94 us
    unnamed x9, local copies, waits for them, and re-layouts  2.49 us
  transfers between devices with their start and end apart: 2, of which 0 were waited for; matrix products, arithmetic and copies ran while one was open for 0% of the time, Pallas kernels for 2%

profile of v1, /device:TPU:0, one launch (start us, length us, event | category | flops | bytes accessed | tf_op | source)
XLA Modules:
  0.0 91.3 jit_solution(14550104525842756003)
XLA Ops:
  0.0 0.8 copy.10.refs_0_.near0_ref
  0.8 2.9 %collective-permute-start.1 = (s32[4,2]{1,0:T(4,128)S(1)}, s32[4,2]{1,0:T(4,128)S(1)}, u32[]{:S(2)}, u32[]{:S(2)}) collective-permute-start(s32[4,2]{1,0:T(4,128)S(1)} %copy.10.refs_0_.near0_ref), channel_id=1, source_target_pairs={{2,0},{3,1},{0,2},{1,3},{6,4},{7,5},{4,6},{5,7},{10,8},{11,9},{8,1... | collective-permute-start | bytes 104 | tf_op jit(solution)/shard_map/ppermute | solution.py:24
  3.7 0.0 collective-permute-start
  3.7 0.0 copy-start
  3.7 1.6 %copy-done = f32[1,2,128,2048]{3,2,1,0:T(8,128)S(1)} copy-done((f32[1,2,128,2048]{3,2,1,0:T(8,128)S(1)}, f32[1,2,128,2048]{3,2,1,0:T(8,128)}, u32[]{:S(2)}) %copy-start) | copy-done | bytes 2097176
  5.3 0.0 copy-start.1
  5.3 1.4 %extract.2.own_blocks = bf16[1,4,2,128,256]{4,3,2,1,0:T(8,128)(2,1)S(1)} custom-call(s32[4,2]{1,0:T(4,128)S(1)} %copy.10.refs_0_.near0_ref, f32[1,2,128,2048]{3,2,1,0:T(8,128)S(1)} %copy-done), custom_call_target="tpu_custom_call" | custom-call | bytes 2097152 | tf_op jit(solution)/shard_map/extract/pallas_call | solution.py:462
  6.7 0.0 copy-start.2
  6.7 0.0 copy-start.3
  6.8 0.0 collective-permute-done.1.refs_1_.near2_ref
  6.8 0.0 collective-permute-done.refs_0_.near1_ref
  6.8 0.1 copy-done.1
  6.9 2.3 %extract.3.blocks = bf16[2,4,2,128,256]{4,3,2,1,0:T(8,128)(2,1)S(1)} custom-call(s32[4,2]{1,0:T(4,128)S(1)} %collective-permute-done.refs_0_.near1_ref, s32[4,2]{1,0:T(4,128)S(1)} %collective-permute-done.1.refs_1_.near2_ref, f32[1,2,128,2048]{3,2,1,0:T(8,128)S(1)} %copy-done.1), custom_call_target="tpu_custom_call" | custom-call | bytes 2097152 | tf_op jit(solution)/shard_map/extract/pallas_call | solution.py:462
  9.2 0.0 copy-done.2
  9.2 0.0 copy-done.3
  9.2 77.5 %windows.1.terms_ref = bf16[3,4,2,128,256]{4,3,2,1,0:T(8,128)(2,1)S(1)} custom-call(s32[4,2]{1,0:T(4,128)S(1)} %copy.10.refs_0_.near0_ref, bf16[1,4,2,128,256]{4,3,2,1,0:T(8,128)(2,1)S(1)} %extract.2.own_blocks, bf16[2,4,2,128,256]{4,3,2,1,0:T(8,128)(2,1)S(1)} %extract.3.blocks, f32[2,2,256,256]{3,2,1,0:T(8,128)S(1)} %copy-done.2, ...), custom_call_target="tpu_custom_call" | custom-call | tf_op jit(solution)/shard_map/windows/pallas_call | solution.py:477
  86.7 4.6 %gather.1 = f32[1,2,128,2048]{3,2,1,0:T(8,128)} custom-call(s32[4,2]{1,0:T(4,128)S(1)} %copy.10.refs_0_.near0_ref, s32[4,2]{1,0:T(4,128)S(1)} %collective-permute-done.refs_0_.near1_ref, s32[4,2]{1,0:T(4,128)S(1)} %collective-permute-done.1.refs_1_.near2_ref, bf16[3,4,2,128,256]{4,3,2,1,0:T(8,128)(2,1)S(1)} %windows.1.terms_ref), custom_call_target="tpu_custom_call" | custom-call | tf_op jit(solution)/shard_map/gather/pallas_call | solution.py:508
Async XLA Ops:
  0.8 6.0 %collective-permute-start.1 = (s32[4,2]{1,0:T(4,128)S(1)}, s32[4,2]{1,0:T(4,128)S(1)}, u32[]{:S(2)}, u32[]{:S(2)}) collective-permute-start(s32[4,2]{1,0:T(4,128)S(1)} %copy.10.refs_0_.near0_ref), channel_id=1, source_target_pairs={{2,0},{3,1},{0,2},{1,3},{6,4},{7,5},{4,6},{5,7},{10,8},{11,9},{8,1... | collective-permute-start | bytes 104 | tf_op jit(solution)/shard_map/ppermute | solution.py:24
  3.7 3.1 %collective-permute-start = (s32[4,2]{1,0:T(4,128)S(1)}, s32[4,2]{1,0:T(4,128)S(1)}, u32[]{:S(2)}, u32[]{:S(2)}) collective-permute-start(s32[4,2]{1,0:T(4,128)S(1)} %copy.10.refs_0_.near0_ref), channel_id=1, source_target_pairs={{3,0},{0,1},{1,2},{2,3},{7,4},{4,5},{5,6},{6,7},{11,8},{8,9},{9,10... | collective-permute-start | bytes 104 | tf_op jit(solution)/shard_map/ppermute | solution.py:24
  3.7 1.6 %copy-start = (f32[1,2,128,2048]{3,2,1,0:T(8,128)S(1)}, f32[1,2,128,2048]{3,2,1,0:T(8,128)}, u32[]{:S(2)}) copy-start(f32[1,2,128,2048]{3,2,1,0:T(8,128)} %refs_2_.1) | copy-start | bytes 6291460
  5.3 1.6 %copy-start.1 = (f32[1,2,128,2048]{3,2,1,0:T(8,128)S(1)}, f32[1,2,128,2048]{3,2,1,0:T(8,128)}, u32[]{:S(2)}) copy-start(f32[1,2,128,2048]{3,2,1,0:T(8,128)} %refs_2_.1) | copy-start | bytes 6291460
  6.7 2.5 %copy-start.2 = (f32[2,2,256,256]{3,2,1,0:T(8,128)S(1)}, f32[2,2,256,256]{3,2,1,0:T(8,128)}, u32[]{:S(2)}) copy-start(f32[2,2,256,256]{3,2,1,0:T(8,128)} %probe_ref.1) | copy-start | bytes 3145732
  6.7 2.5 %copy-start.3 = (f32[4,256,256]{2,1,0:T(8,128)S(1)}, f32[4,256,256]{2,1,0:T(8,128)}, u32[]{:S(2)}) copy-start(f32[4,256,256]{2,1,0:T(8,128)} %measured_ref.1) | copy-start | bytes 3145732

commit v2 on v1

--- a/solution.py
+++ b/solution.py
@@ -255,16 +255,11 @@
     def _(turn):
         rows_out(order(turn)).start()
 
-    @pl.loop(0, count)
-    def _(turn):
-        block_out(1, order(turn)).start()
-
     def upper(k):
         keep = tile_rows - lax.rem(near0_ref[k, 0], tile_rows)
         return upper_rows((tile_rows, pixels), keep)
 
-    @pl.loop(0, count)
-    def _(turn):
+    def merge_and_send(turn):
         k = order(turn)
         rows_out(k).wait_recv()
         for part in range(2):
@@ -282,6 +277,15 @@
         @pl.when(jnp.logical_not(own))
         def _():
             block_out(0, k).start()
+
+    half = (count + 1) // 2
+    for begin, end in ((0, half), (half, count)):
+
+        @pl.loop(begin, end)
+        def _(turn):
+            block_out(1, order(turn)).start()
+
+        pl.loop(begin, end)(merge_and_send)
 
     def term_out(s, j):
         return pltpu.make_async_remote_copy(

time: 91.5 us -> 91.8 us (level)
  no operation moved by 1% of the time
where the time goes in v2:
time: 91.8 us; the launch traced here: 91.7 us
  Pallas kernels  86.1 us (94%)
  starting transfers between devices  2.94 us (3%)
  local copies, waits for them, and re-layouts  2.49 us (3%)
    pallas_call x1, Pallas kernels, on_device(): pl.pallas_call(functools.partial(main_kernel, count, sections, lats), out...  77.8 us
    pallas_call x1, Pallas kernels, on_device(): pl.pallas_call(gather_kernel, out_shape=jax.ShapeDtypeStruct(object_slice...  4.64 us
    pallas_call x2, Pallas kernels, extract(): pl.pallas_call(extract_kernel, out_shape=jax.ShapeDtypeStruct((len(places...  3.72 us
    ppermute x2, starting transfers between devices, shifted(): return lax.ppermute(block, axis, route)  2.94 us
    unnamed x9, local copies, waits for them, and re-layouts  2.49 us
  transfers between devices with their start and end apart: 2, of which 0 were waited for; matrix products, arithmetic and copies ran while one was open for 0% of the time, Pallas kernels for 2%

profile of v2, /device:TPU:0, one launch (start us, length us, event | category | flops | bytes accessed | tf_op | source)
XLA Modules:
  0.0 91.7 jit_solution(17028989475861413882)
XLA Ops:
  0.0 0.8 copy.10.refs_0_.near0_ref
  0.8 2.9 %collective-permute-start.1 = (s32[4,2]{1,0:T(4,128)S(1)}, s32[4,2]{1,0:T(4,128)S(1)}, u32[]{:S(2)}, u32[]{:S(2)}) collective-permute-start(s32[4,2]{1,0:T(4,128)S(1)} %copy.10.refs_0_.near0_ref), channel_id=1, source_target_pairs={{2,0},{3,1},{0,2},{1,3},{6,4},{7,5},{4,6},{5,7},{10,8},{11,9},{8,1... | collective-permute-start | bytes 104 | tf_op jit(solution)/shard_map/ppermute | solution.py:24
  3.7 0.0 collective-permute-start
  3.7 0.0 copy-start
  3.7 1.6 %copy-done = f32[1,2,128,2048]{3,2,1,0:T(8,128)S(1)} copy-done((f32[1,2,128,2048]{3,2,1,0:T(8,128)S(1)}, f32[1,2,128,2048]{3,2,1,0:T(8,128)}, u32[]{:S(2)}) %copy-start) | copy-done | bytes 2097176
  5.3 0.0 copy-start.1
  5.3 1.4 %extract.2.own_blocks = bf16[1,4,2,128,256]{4,3,2,1,0:T(8,128)(2,1)S(1)} custom-call(s32[4,2]{1,0:T(4,128)S(1)} %copy.10.refs_0_.near0_ref, f32[1,2,128,2048]{3,2,1,0:T(8,128)S(1)} %copy-done), custom_call_target="tpu_custom_call" | custom-call | bytes 2097152 | tf_op jit(solution)/shard_map/extract/pallas_call | solution.py:466
  6.7 0.0 copy-start.2
  6.7 0.0 copy-start.3
  6.8 0.0 collective-permute-done.1.refs_1_.near2_ref
  6.8 0.0 collective-permute-done.refs_0_.near1_ref
  6.8 0.1 copy-done.1
  6.9 2.3 %extract.3.blocks = bf16[2,4,2,128,256]{4,3,2,1,0:T(8,128)(2,1)S(1)} custom-call(s32[4,2]{1,0:T(4,128)S(1)} %collective-permute-done.refs_0_.near1_ref, s32[4,2]{1,0:T(4,128)S(1)} %collective-permute-done.1.refs_1_.near2_ref, f32[1,2,128,2048]{3,2,1,0:T(8,128)S(1)} %copy-done.1), custom_call_target="tpu_custom_call" | custom-call | bytes 2097152 | tf_op jit(solution)/shard_map/extract/pallas_call | solution.py:466
  9.2 0.0 copy-done.2
  9.2 0.0 copy-done.3
  9.2 77.8 %windows.1.terms_ref = bf16[3,4,2,128,256]{4,3,2,1,0:T(8,128)(2,1)S(1)} custom-call(s32[4,2]{1,0:T(4,128)S(1)} %copy.10.refs_0_.near0_ref, bf16[1,4,2,128,256]{4,3,2,1,0:T(8,128)(2,1)S(1)} %extract.2.own_blocks, bf16[2,4,2,128,256]{4,3,2,1,0:T(8,128)(2,1)S(1)} %extract.3.blocks, f32[2,2,256,256]{3,2,1,0:T(8,128)S(1)} %copy-done.2, ...), custom_call_target="tpu_custom_call" | custom-call | tf_op jit(solution)/shard_map/windows/pallas_call | solution.py:481
  87.0 4.6 %gather.1 = f32[1,2,128,2048]{3,2,1,0:T(8,128)} custom-call(s32[4,2]{1,0:T(4,128)S(1)} %copy.10.refs_0_.near0_ref, s32[4,2]{1,0:T(4,128)S(1)} %collective-permute-done.refs_0_.near1_ref, s32[4,2]{1,0:T(4,128)S(1)} %collective-permute-done.1.refs_1_.near2_ref, bf16[3,4,2,128,256]{4,3,2,1,0:T(8,128)(2,1)S(1)} %windows.1.terms_ref), custom_call_target="tpu_custom_call" | custom-call | tf_op jit(solution)/shard_map/gather/pallas_call | solution.py:512
Async XLA Ops:
  0.8 6.0 %collective-permute-start.1 = (s32[4,2]{1,0:T(4,128)S(1)}, s32[4,2]{1,0:T(4,128)S(1)}, u32[]{:S(2)}, u32[]{:S(2)}) collective-permute-start(s32[4,2]{1,0:T(4,128)S(1)} %copy.10.refs_0_.near0_ref), channel_id=1, source_target_pairs={{2,0},{3,1},{0,2},{1,3},{6,4},{7,5},{4,6},{5,7},{10,8},{11,9},{8,1... | collective-permute-start | bytes 104 | tf_op jit(solution)/shard_map/ppermute | solution.py:24
  3.7 3.1 %collective-permute-start = (s32[4,2]{1,0:T(4,128)S(1)}, s32[4,2]{1,0:T(4,128)S(1)}, u32[]{:S(2)}, u32[]{:S(2)}) collective-permute-start(s32[4,2]{1,0:T(4,128)S(1)} %copy.10.refs_0_.near0_ref), channel_id=1, source_target_pairs={{3,0},{0,1},{1,2},{2,3},{7,4},{4,5},{5,6},{6,7},{11,8},{8,9},{9,10... | collective-permute-start | bytes 104 | tf_op jit(solution)/shard_map/ppermute | solution.py:24
  3.7 1.6 %copy-start = (f32[1,2,128,2048]{3,2,1,0:T(8,128)S(1)}, f32[1,2,128,2048]{3,2,1,0:T(8,128)}, u32[]{:S(2)}) copy-start(f32[1,2,128,2048]{3,2,1,0:T(8,128)} %refs_2_.1) | copy-start | bytes 6291460
  5.3 1.6 %copy-start.1 = (f32[1,2,128,2048]{3,2,1,0:T(8,128)S(1)}, f32[1,2,128,2048]{3,2,1,0:T(8,128)}, u32[]{:S(2)}) copy-start(f32[1,2,128,2048]{3,2,1,0:T(8,128)} %refs_2_.1) | copy-start | bytes 6291460
  6.7 2.5 %copy-start.2 = (f32[2,2,256,256]{3,2,1,0:T(8,128)S(1)}, f32[2,2,256,256]{3,2,1,0:T(8,128)}, u32[]{:S(2)}) copy-start(f32[2,2,256,256]{3,2,1,0:T(8,128)} %probe_ref.1) | copy-start | bytes 3145732
  6.7 2.5 %copy-start.3 = (f32[4,256,256]{2,1,0:T(8,128)S(1)}, f32[4,256,256]{2,1,0:T(8,128)}, u32[]{:S(2)}) copy-start(f32[4,256,256]{2,1,0:T(8,128)} %measured_ref.1) | copy-start | bytes 3145732

commit v3 on v1

--- a/solution.py
+++ b/solution.py
@@ -60,7 +60,7 @@
 
     for j in range(len(near)):
 
-        @pl.loop(0, count)
+        @pl.loop(0, count, unroll=True)
         def _(k):
             row, first, shift = window_place(near[j], k, tile_rows, cols // LANES)
             start = pl.multiple_of(first * LANES, LANES)
@@ -80,7 +80,7 @@
 
     for j in range(TILES):
 
-        @pl.loop(0, count)
+        @pl.loop(0, count, unroll=True)
         def _(k):
             row, first, shift = window_place(near[j], k, tile_rows, cols // LANES)
             start = pl.multiple_of(first * LANES, LANES)

time: 91.5 us -> 90.4 us (0.988)
  Pallas kernels: 85.8 us -> 84.4 us
  transfers between devices with their start and end apart: 2 -> 2, of which waited for: 0 -> 1; matrix products, arithmetic and copies ran while one was open for 0% -> 0% of each run, Pallas kernels for 2% -> 1%
where the time goes in v3:
time: 90.4 us; the launch traced here: 90.2 us
  Pallas kernels  84.4 us (93%)
  starting transfers between devices  2.94 us (3%)
  local copies, waits for them, and re-layouts  2.54 us (3%)
    pallas_call x1, Pallas kernels, on_device(): pl.pallas_call(functools.partial(main_kernel, count, sections, lats), out...  77.4 us
    pallas_call x1, Pallas kernels, on_device(): pl.pallas_call(gather_kernel, out_shape=jax.ShapeDtypeStruct(object_slice...  4.2 us
    ppermute x2, starting transfers between devices, shifted(): return lax.ppermute(block, axis, route)  2.94 us
    pallas_call x2, Pallas kernels, extract(): pl.pallas_call(extract_kernel, out_shape=jax.ShapeDtypeStruct((len(places...  2.81 us
    unnamed x9, local copies, waits for them, and re-layouts  2.54 us
  transfers between devices with their start and end apart: 2, of which 1 were waited for; matrix products, arithmetic and copies ran while one was open for 0% of the time, Pallas kernels for 1%

profile of v3, /device:TPU:0, one launch (start us, length us, event | category | flops | bytes accessed | tf_op | source)
XLA Modules:
  0.0 90.2 jit_solution(5960947786084075610)
XLA Ops:
  0.0 0.8 copy.10.refs_0_.near0_ref
  0.8 2.9 %collective-permute-start.1 = (s32[4,2]{1,0:T(4,128)S(1)}, s32[4,2]{1,0:T(4,128)S(1)}, u32[]{:S(2)}, u32[]{:S(2)}) collective-permute-start(s32[4,2]{1,0:T(4,128)S(1)} %copy.10.refs_0_.near0_ref), channel_id=1, source_target_pairs={{2,0},{3,1},{0,2},{1,3},{6,4},{7,5},{4,6},{5,7},{10,8},{11,9},{8,1... | collective-permute-start | bytes 104 | tf_op jit(solution)/shard_map/ppermute | solution.py:24
  3.7 0.0 collective-permute-start
  3.7 0.0 copy-start
  3.7 1.6 %copy-done = f32[1,2,128,2048]{3,2,1,0:T(8,128)S(1)} copy-done((f32[1,2,128,2048]{3,2,1,0:T(8,128)S(1)}, f32[1,2,128,2048]{3,2,1,0:T(8,128)}, u32[]{:S(2)}) %copy-start) | copy-done | bytes 2097176
  5.3 0.0 copy-start.1
  5.3 1.1 %extract.2.own_blocks = bf16[1,4,2,128,256]{4,3,2,1,0:T(8,128)(2,1)S(1)} custom-call(s32[4,2]{1,0:T(4,128)S(1)} %copy.10.refs_0_.near0_ref, f32[1,2,128,2048]{3,2,1,0:T(8,128)S(1)} %copy-done), custom_call_target="tpu_custom_call" | custom-call | bytes 2097152 | tf_op jit(solution)/shard_map/extract/pallas_call | solution.py:462
  6.5 0.0 copy-start.2
  6.5 0.0 copy-start.3
  6.5 0.0 collective-permute-done.1.refs_1_.near2_ref
  6.5 0.2 collective-permute-done.refs_0_.near1_ref
  6.7 0.2 copy-done.1
  6.9 1.7 %extract.3.blocks = bf16[2,4,2,128,256]{4,3,2,1,0:T(8,128)(2,1)S(1)} custom-call(s32[4,2]{1,0:T(4,128)S(1)} %collective-permute-done.refs_0_.near1_ref, s32[4,2]{1,0:T(4,128)S(1)} %collective-permute-done.1.refs_1_.near2_ref, f32[1,2,128,2048]{3,2,1,0:T(8,128)S(1)} %copy-done.1), custom_call_target="tpu_custom_call" | custom-call | bytes 2097152 | tf_op jit(solution)/shard_map/extract/pallas_call | solution.py:462
  8.6 0.0 copy-done.2
  8.6 0.0 copy-done.3
  8.6 77.4 %windows.1.terms_ref = bf16[3,4,2,128,256]{4,3,2,1,0:T(8,128)(2,1)S(1)} custom-call(s32[4,2]{1,0:T(4,128)S(1)} %copy.10.refs_0_.near0_ref, bf16[1,4,2,128,256]{4,3,2,1,0:T(8,128)(2,1)S(1)} %extract.2.own_blocks, bf16[2,4,2,128,256]{4,3,2,1,0:T(8,128)(2,1)S(1)} %extract.3.blocks, f32[2,2,256,256]{3,2,1,0:T(8,128)S(1)} %copy-done.2, ...), custom_call_target="tpu_custom_call" | custom-call | tf_op jit(solution)/shard_map/windows/pallas_call | solution.py:477
  86.0 4.2 %gather.1 = f32[1,2,128,2048]{3,2,1,0:T(8,128)} custom-call(s32[4,2]{1,0:T(4,128)S(1)} %copy.10.refs_0_.near0_ref, s32[4,2]{1,0:T(4,128)S(1)} %collective-permute-done.refs_0_.near1_ref, s32[4,2]{1,0:T(4,128)S(1)} %collective-permute-done.1.refs_1_.near2_ref, bf16[3,4,2,128,256]{4,3,2,1,0:T(8,128)(2,1)S(1)} %windows.1.terms_ref), custom_call_target="tpu_custom_call" | custom-call | tf_op jit(solution)/shard_map/gather/pallas_call | solution.py:508
Async XLA Ops:
  0.8 5.7 %collective-permute-start.1 = (s32[4,2]{1,0:T(4,128)S(1)}, s32[4,2]{1,0:T(4,128)S(1)}, u32[]{:S(2)}, u32[]{:S(2)}) collective-permute-start(s32[4,2]{1,0:T(4,128)S(1)} %copy.10.refs_0_.near0_ref), channel_id=1, source_target_pairs={{2,0},{3,1},{0,2},{1,3},{6,4},{7,5},{4,6},{5,7},{10,8},{11,9},{8,1... | collective-permute-start | bytes 104 | tf_op jit(solution)/shard_map/ppermute | solution.py:24
  3.7 3.0 %collective-permute-start = (s32[4,2]{1,0:T(4,128)S(1)}, s32[4,2]{1,0:T(4,128)S(1)}, u32[]{:S(2)}, u32[]{:S(2)}) collective-permute-start(s32[4,2]{1,0:T(4,128)S(1)} %copy.10.refs_0_.near0_ref), channel_id=1, source_target_pairs={{3,0},{0,1},{1,2},{2,3},{7,4},{4,5},{5,6},{6,7},{11,8},{8,9},{9,10... | collective-permute-start | bytes 104 | tf_op jit(solution)/shard_map/ppermute | solution.py:24
  3.7 1.6 %copy-start = (f32[1,2,128,2048]{3,2,1,0:T(8,128)S(1)}, f32[1,2,128,2048]{3,2,1,0:T(8,128)}, u32[]{:S(2)}) copy-start(f32[1,2,128,2048]{3,2,1,0:T(8,128)} %refs_2_.1) | copy-start | bytes 6291460
  5.3 1.6 %copy-start.1 = (f32[1,2,128,2048]{3,2,1,0:T(8,128)S(1)}, f32[1,2,128,2048]{3,2,1,0:T(8,128)}, u32[]{:S(2)}) copy-start(f32[1,2,128,2048]{3,2,1,0:T(8,128)} %refs_2_.1) | copy-start | bytes 6291460
  6.5 2.1 %copy-start.2 = (f32[2,2,256,256]{3,2,1,0:T(8,128)S(1)}, f32[2,2,256,256]{3,2,1,0:T(8,128)}, u32[]{:S(2)}) copy-start(f32[2,2,256,256]{3,2,1,0:T(8,128)} %probe_ref.1) | copy-start | bytes 3145732
  6.5 2.1 %copy-start.3 = (f32[4,256,256]{2,1,0:T(8,128)S(1)}, f32[4,256,256]{2,1,0:T(8,128)}, u32[]{:S(2)}) copy-start(f32[4,256,256]{2,1,0:T(8,128)} %measured_ref.1) | copy-start | bytes 3145732
